TPU v7x, 256 devices: a whole 4x4x8 slice. The times are simulated.
256 devices in a mesh: section: 4 (over x), dp: 8 (over z_hi, core), tp: 8 (over z_lo, y).
Axes of the slice: x: 4, y: 4, z: 8 (z_hi: 4, z_lo: 2; z = z_hi * 2 + z_lo), core: 2. Of those that a mesh axis runs over, the one named last changes fastest.
Arguments:
- rollout_rows: bfloat16 [1536, 4096], P(('section', 'tp'), 'dp'), may hold values from -6 to 6
- segment_ids: int32 [1536], P(('section', 'tp')), may hold values from 0 to 11, never falling along the last dimension, each value on 1 to 768 neighbouring positions
- gate_weights: bfloat16 [4, 4096, 14336], P('section', 'dp', 'tp'), may hold values from -0.09375 to 0.09375
- up_weights: bfloat16 [4, 4096, 14336], P('section', 'dp', 'tp'), may hold values from -0.09375 to 0.09375
- down_weights: bfloat16 [4, 14336, 4096], P('section', 'tp', 'dp'), may hold values from -0.046875 to 0.046875
- head_weights: bfloat16 [4, 4096], P('section', 'dp'), may hold values from -0.09375 to 0.09375
Outputs:
- advantages: float32 [1536], P(('section', 'tp'))
- returns: float32 [1536], P(('section', 'tp'))
Inputs may be any that keep to these rules, and one draw needn't show every extreme that they name: `segment_ids`: ids never fall along the pack; each response holds 1 to 768 consecutive rows, one exactly 768; all 12 responses occur.
All inputs are finite; a program needn't handle non-finite values.
Results may differ from a plain program's by a relative error of at most 0.00076.
Values may be sent and summed in bfloat16 or wider, within the bound.
No kernel may reach another device: no remote copies, remote signals or barrier semaphores. Data moves between devices by JAX's collectives and lax.ppermute only.
A program may use at most 128 MiB of HBM per device.

v0:
```python
import jax
import jax.numpy as jnp
from jax import lax
from jax.sharding import PartitionSpec as P

epsilon = 1e-05
kl_coef = 0.2
discount = 1.0
trace_decay = 1.0


def from_behind(block, axis, distance):
    devices = range(lax.axis_size(axis))
    route = [(i - distance, i) for i in devices if i - distance in devices]
    return lax.ppermute(block, axis, route)


def entering(shard, axis, combine, identity):
    devices, here = (lax.axis_size(axis), lax.axis_index(axis))
    everything = jax.tree.map(lambda part: lax.all_gather(part, axis), shard)
    start = jax.tree.map(
        lambda part, zero: jnp.broadcast_to(jnp.asarray(zero, part.dtype), part.shape),
        shard,
        identity,
    )

    def lap(k, before):
        at = devices - 1 - k
        reached = at > here
        new = combine(before, jax.tree.map(lambda part: part[at], everything))
        return jax.tree.map(lambda a, b: jnp.where(reached, a, b), new, before)

    return lax.fori_loop(0, devices, lap, start)


def shards(rollout_rows, segment_ids, gate_weights, up_weights, down_weights, head_weights):
    sections = lax.axis_size("section")
    tensor_ways = lax.axis_size("tp")
    owners = lax.axis_size("dp")
    block_rows = rollout_rows.shape[0]
    width_part = rollout_rows.shape[1]
    arrived = lax.all_gather(rollout_rows, ("section", "tp"), axis=0, tiled=True)
    ordered = (
        arrived.reshape(sections, tensor_ways, block_rows, width_part)
        .transpose(1, 0, 2, 3)
        .reshape(-1, width_part)
    )
    gate_part = gate_weights[0]
    up_part = up_weights[0]
    units = gate_part.shape[1]
    summed = lax.psum_scatter(
        jnp.concatenate(
            (
                jnp.dot(ordered, gate_part, preferred_element_type=jnp.float32),
                jnp.dot(ordered, up_part, preferred_element_type=jnp.float32),
            ),
            axis=1,
        ),
        "dp",
        scatter_dimension=0,
        tiled=True,
    )
    gate_sum = summed[:, :units]
    up_sum = summed[:, units:]
    hidden = (jax.nn.silu(gate_sum) * up_sum).astype(jnp.bfloat16)
    down_part = down_weights[0]
    projected = jnp.dot(
        lax.all_gather(hidden, "dp", axis=0, tiled=True),
        down_part,
        preferred_element_type=jnp.float32,
    )
    mixed = lax.psum_scatter(projected, "tp", scatter_dimension=0, tiled=True)
    own_rows = mixed.shape[0]
    residual = lax.dynamic_slice_in_dim(ordered, lax.axis_index("tp") * own_rows, own_rows, 0)
    stream = residual.astype(jnp.float32) + mixed
    head_part = head_weights[0].astype(jnp.float32)
    squares, along = lax.psum(
        (jnp.sum(stream * stream, axis=1), jnp.sum(stream * head_part, axis=1)), "dp"
    )
    scores = along / jnp.sqrt(squares / (width_part * owners) + epsilon)
    joined = lax.all_to_all(
        scores.reshape(sections, block_rows), "section", split_axis=0, concat_axis=0, tiled=True
    )
    policy_score = joined[0]
    ref_score = joined[1]
    reward_score = joined[2]
    values = joined[3]
    segments = segment_ids.astype(jnp.float32)
    next_value, next_segment = from_behind((values[:1], segments[:1]), ("section", "tp"), -1)
    later_values = jnp.concatenate((values[1:], next_value))
    later_segments = jnp.concatenate((segments[1:], next_segment))
    same = (later_segments == segments).astype(jnp.float32)
    rewards = -kl_coef * (policy_score - ref_score) + (1.0 - same) * reward_score
    deltas = rewards + discount * later_values * same - values
    factors = discount * trace_decay * same

    def advance(carried, inputs):
        delta_now, factor_now = inputs
        updated = delta_now + factor_now * carried
        return (updated, updated)

    final_state, local_advantage = lax.scan(
        advance, jnp.float32(0.0), (deltas, factors), reverse=True
    )
    products = jnp.cumprod(factors[::-1])[::-1]

    def compose(earlier, later):
        return (later[0] + later[1] * earlier[0], later[1] * earlier[1])

    incoming, through = entering(
        (local_advantage[0], products[0]),
        ("section", "tp"),
        compose,
        (jnp.float32(0.0), jnp.float32(1.0)),
    )
    advantages = local_advantage + products * incoming
    return (advantages, advantages + values)


def solution(mesh):
    return jax.shard_map(
        shards,
        mesh=mesh,
        in_specs=(
            P(("section", "tp"), "dp"),
            P(("section", "tp")),
            P("section", "dp", "tp"),
            P("section", "dp", "tp"),
            P("section", "tp", "dp"),
            P("section", "dp"),
        ),
        out_specs=(P(("section", "tp")), P(("section", "tp"))),
        check_vma=False,
    )
```

profile of v0, /device:TPU:8, one launch (start us, length us, event | category | flops | bytes accessed | tf_op | source)
XLA Modules:
  0.0 848.5 jit_solution(421732016931791345)
XLA Ops:
  8.0 159.3 %all-gather.4.cloned.1.call-done = bf16[1536,512]{1,0:T(8,128)(2,1)} async-done(((bf16[48,512]{1,0:T(8,128)(2,1)}), bf16[1536,512]{1,0:T(8,128)(2,1)}) %all-gather.4.cloned.1.call-update) | async-done | bytes 1572880 | tf_op jit(solution)/shard_map/all_gather | solution.py:42
  167.2 1.5 copy.10
  168.8 3.0 fusion.2
  171.8 3.0 fusion.4
  174.9 8.0 pad_maximum_fusion
  183.0 225.0 %reduce-scatter.3.cloned.1.call-done = f32[192,3584]{1,0:T(8,128)} async-done(((f32[1536,3584]{1,0:T(8,128)}), f32[192,3584]{1,0:T(8,128)}) %reduce-scatter.3.cloned.1.call-update) | async-done | bytes 2752528 | tf_op jit(solution)/shard_map/reduce_scatter | solution.py:51
  408.0 3.0 fusion.6
  411.1 63.9 %all-gather.6.cloned.1.call-done = bf16[1536,1792]{1,0:T(8,128)(2,1)} async-done(((bf16[192,1792]{1,0:T(8,128)(2,1)}), bf16[1536,1792]{1,0:T(8,128)(2,1)}) %all-gather.6.cloned.1.call-update) | async-done | bytes 5505040 | tf_op jit(solution)/shard_map/all_gather | solution.py:68
  475.0 7.8 fusion
  483.5 2.8 collective-permute-start
  487.1 1.9 collective-permute-done
  489.8 42.0 %reduce-scatter.5.cloned.1.call-done = f32[192,512]{1,0:T(8,128)} async-done(((f32[1536,512]{1,0:T(8,128)}), f32[192,512]{1,0:T(8,128)}) %reduce-scatter.5.cloned.1.call-update) | async-done | bytes 393232 | tf_op jit(solution)/shard_map/reduce_scatter | solution.py:72
  531.8 1.2 multiply_reduce_fusion
  532.9 14.2 %all-reduce.3 = (f32[192]{0:T(256)S(1)}, f32[192]{0:T(256)S(1)}) all-reduce(f32[192]{0:T(256)S(1)} %get-tuple-element.240, f32[192]{0:T(256)S(1)} %get-tuple-element.239), channel_id=1, replica_groups=mesh['section'=4,'dp'=8,'tp'=8] {'dp'}, use_global_device_ids=true, to_apply=%region_3.4 | all-reduce | flops 384 | bytes 3072 | tf_op jit(solution)/shard_map/psum | solution.py:77
  547.8 4.1 all-to-all-start
  552.8 1.3 bitcast_dynamic-update-slice_fusion
  554.1 3.1 all-to-all-done
  557.3 3.9 collective-permute-start.1
  561.2 1.7 collective-permute-done.1
  562.8 0.7 bitcast_subtract_fusion
  563.5 118.4 %while.31 = (s32[]{:T(128)}, f32[]{:T(128)}, f32[48]{0:T(128)S(1)}, f32[48]{0:T(128)S(1)}, f32[48]{0:T(128)S(1)}, /*index=5*/s32[]{:T(128)}, s32[]{:T(128)}) while((s32[]{:T(128)}, f32[]{:T(128)}, f32[48]{0:T(128)S(1)}, f32[48]{0:T(128)S(1)}, f32[48]{0:T(128)S(1)}, /*index=5*/s32[]{:T(128)}, s32[]{:T(128)}) %tuple.72), condition=%wide.region_7.8_spmd, body=%wide.region_6.7_spmd.sunk | while | flops 5 | bytes 157 | solution.py:102
  681.9 0.8 slice_dynamic-update-slice_fusion
  682.7 78.8 %all-reduce.2 = (f32[32]{0:T(128)S(1)}, f32[32]{0:T(128)S(1)}) all-reduce(f32[32]{0:T(128)S(1)} %slice_dynamic-update-slice_fusion, f32[32]{0:T(128)S(1)} %bitcast_dynamic-update-slice_fusion), channel_id=1, replica_groups=mesh['section'=4,'dp'=8,'tp'=8] {'section','tp'}, use_global_device_ids=true, to_apply=%add | all-reduce | flops 64 | bytes 512
  761.4 80.0 %while.32 = (s32[]{:T(128)}, f32[]{:T(128)}, s32[]{:T(128)}, f32[32]{0:T(128)S(1)}, f32[32]{0:T(128)S(1)}, /*index=5*/s32[]{:T(128)}, s32[]{:T(128)}, s32[]{:T(128)}, s32[]{:T(128)}) while((s32[]{:T(128)}, f32[]{:T(128)}, s32[]{:T(128)}, f32[32]{0:T(128)S(1)}, f32[32]{0:T(128)S(1)}, /*index=5*/s32[]{:T(128)}, s32[]{:T(128)}, s32[]{:T(128)}, ...), condition=%wide.region_10.11_spmd, body=%wide.region_9.10_spmd.sunk | while | flops 10 | bytes 217 | solution.py:33
  (245 shorter events, 104.1 us)
Async XLA Ops:
  7.2 161.6 %copy-start = (bf16[1,512,1792]{2,1,0:T(8,128)(2,1)S(1)}, bf16[1,512,1792]{2,1,0:T(8,128)(2,1)}, u32[]{:S(2)}) copy-start(bf16[1,512,1792]{2,1,0:T(8,128)(2,1)} %param.13) | copy-start | bytes 5505028
  7.2 160.1 %all-gather.4.cloned.1.call-start = ((), (), s32[]{:S(2)}) async-start(), calls=%async_computation.3 | async-start | bytes 1622016 | tf_op jit(solution)/shard_map/all_gather | solution.py:42
  7.9 400.1 %reduce-scatter.3.cloned.1.call-start = ((), (), s32[]{:S(2)}) async-start(), calls=%async_computation.4 | async-start | bytes 24772608 | tf_op jit(solution)/shard_map/reduce_scatter | solution.py:51
  168.8 3.0 copy-start.3
  182.9 292.1 %all-gather.6.cloned.1.call-start = ((), (), s32[]{:S(2)}) async-start(), calls=%async_computation.5 | async-start | bytes 6193152 | tf_op jit(solution)/shard_map/all_gather | solution.py:68
  411.1 120.7 %reduce-scatter.5.cloned.1.call-start = ((), (), s32[]{:S(2)}) async-start(), calls=%async_computation.6 | async-start | bytes 3538944 | tf_op jit(solution)/shard_map/reduce_scatter | solution.py:72
  482.8 0.7 copy-start.2
  482.8 3.6 copy-start.1
  482.8 3.6 copy-start.4
  483.5 5.5 collective-permute-start
  547.8 9.4 %all-to-all-start = ((f32[4,1,48]{2,1,0:T(1,128)}), f32[4,1,48]{2,1,0:T(1,128)S(1)}, u32[]{:S(2)}, u32[]{:S(2)}) async-start(f32[4,1,48]{2,1,0:T(1,128)} %all_to_all.6), calls=%async_computation.2 | async-start | bytes 4096 | tf_op jit(solution)/shard_map/all_to_all | solution.py:81
  557.3 5.5 collective-permute-start.1
Sparse Core Ops, SparseCore 0:
  9.8 157.3 all-gather.3
  183.1 224.9 reduce-scatter.2
  411.2 63.8 all-gather.5
  483.0 48.7 reduce-scatter.4
where the time goes:
time: 850 us; the launch traced here: 848 us
  waiting for transfers between devices  498 us (59%)
  local copies, waits for them, and re-layouts  105 us (12%)
  loops' own time  99.4 us (12%)
  blocking collectives  93 us (11%)
  other arithmetic  14.3 us (2%)
  matrix products  13.9 us (2%)
  between operations  13.9 us (2%)
  starting transfers between devices  11 us (1%)
    reduce_scatter x1, waiting for transfers between devices, shards(): lax.psum_scatter(jnp.concatenate((jnp.dot(ordered, gate_part, preferred_e...  225 us
    all_gather x1, waiting for transfers between devices, shards(): lax.all_gather(rollout_rows, ('section', 'tp'), axis=0, tiled=True)  159 us
    unnamed x1, blocking collectives  78.8 us
    all_gather x1, waiting for transfers between devices, shards(): lax.all_gather(hidden, 'dp', axis=0, tiled=True)  63.9 us
    another operation x1, loops' own time, shards(): lax.scan(advance, jnp.float32(0.0), (deltas, factors), reverse=True)  56.9 us
    dynamic_slice x96, local copies, waits for them, and re-layouts, shards(): lax.scan(advance, jnp.float32(0.0), (deltas, factors), reverse=True)  56 us
    another operation x1, loops' own time, entering(): return lax.fori_loop(0, devices, lap, start)  42.6 us
    reduce_scatter x1, waiting for transfers between devices, shards(): mixed = lax.psum_scatter(projected, 'tp', scatter_dimension=0, tiled=True)  42 us
  transfers between devices with their start and end apart: 7, of which 7 were waited for; matrix products, arithmetic and copies ran while one was open for 0% of the time, Pallas kernels for 0%

commit v1 on v0

--- a/solution.py
+++ b/solution.py
@@ -65,7 +65,9 @@
     hidden = (jax.nn.silu(gate_sum) * up_sum).astype(jnp.bfloat16)
     down_part = down_weights[0]
     projected = jnp.dot(
-        lax.all_gather(hidden, "dp", axis=0, tiled=True),
+        jnp.concatenate(
+            lax.all_to_all(jnp.stack([hidden] * lax.axis_size("dp")), "dp", 0, 0), axis=0
+        ),
         down_part,
         preferred_element_type=jnp.float32,
     )

time: 850 us -> 917 us (1.079)
  blocking collectives: 93 us -> 222 us
  waiting for transfers between devices: 498 us -> 435 us
    all_to_all x0 -> x1, blocking collectives: none -> 129 us  [shards(): lax.all_to_all(jnp.stack([hidden] * lax.axis_size('dp')), 'dp', 0, 0)]
    all_gather x1 -> x0, waiting for transfers between devices: 63.9 us -> none  [shards(): lax.all_gather(hidden, 'dp', axis=0, tiled=True)]
  transfers between devices with their start and end apart: 7 -> 6, of which waited for: 7 -> 6; matrix products, arithmetic and copies ran while one was open for 0% -> 0% of each run, Pallas kernels for 0% -> 0%
where the time goes in v1:
time: 917 us; the launch traced here: 914 us
  waiting for transfers between devices  435 us (47%)
  blocking collectives  222 us (24%)
  local copies, waits for them, and re-layouts  108 us (12%)
  loops' own time  102 us (11%)
  between operations  13.9 us (2%)
  other arithmetic  13.4 us (1%)
  matrix products  10.7 us (1%)
  starting transfers between devices  9.85 us (1%)
    reduce_scatter x1, waiting for transfers between devices, shards(): lax.psum_scatter(jnp.concatenate((jnp.dot(ordered, gate_part, preferred_e...  228 us
    all_gather x1, waiting for transfers between devices, shards(): lax.all_gather(rollout_rows, ('section', 'tp'), axis=0, tiled=True)  159 us
    all_to_all x1, blocking collectives, shards(): lax.all_to_all(jnp.stack([hidden] * lax.axis_size('dp')), 'dp', 0, 0)  129 us
    unnamed x1, blocking collectives  78.2 us
    another operation x1, loops' own time, shards(): lax.scan(advance, jnp.float32(0.0), (deltas, factors), reverse=True)  59.2 us
    dynamic_slice x96, local copies, waits for them, and re-layouts, shards(): lax.scan(advance, jnp.float32(0.0), (deltas, factors), reverse=True)  57.8 us
    another operation x1, loops' own time, entering(): return lax.fori_loop(0, devices, lap, start)  42.6 us
    reduce_scatter x1, waiting for transfers between devices, shards(): mixed = lax.psum_scatter(projected, 'tp', scatter_dimension=0, tiled=True)  38.9 us
  transfers between devices with their start and end apart: 6, of which 6 were waited for; matrix products, arithmetic and copies ran while one was open for 0% of the time, Pallas kernels for 0%

profile of v1, /device:TPU:8, one launch (start us, length us, event | category | flops | bytes accessed | tf_op | source)
XLA Modules:
  0.0 913.8 jit_solution(10745488294838461597)
XLA Ops:
  8.0 159.3 %all-gather.3.cloned.1.call-done = bf16[1536,512]{1,0:T(8,128)(2,1)} async-done(((bf16[48,512]{1,0:T(8,128)(2,1)}), bf16[1536,512]{1,0:T(8,128)(2,1)}) %all-gather.3.cloned.1.call-update) | async-done | bytes 1572880 | tf_op jit(solution)/shard_map/all_gather | solution.py:42
  167.2 1.5 copy.10
  168.8 3.0 fusion.2
  171.8 3.0 fusion.4
  174.9 8.0 pad_maximum_fusion
  183.0 228.1 %reduce-scatter.3.cloned.1.call-done = f32[192,3584]{1,0:T(8,128)} async-done(((f32[1536,3584]{1,0:T(8,128)}), f32[192,3584]{1,0:T(8,128)}) %reduce-scatter.3.cloned.1.call-update) | async-done | bytes 2752528 | tf_op jit(solution)/shard_map/reduce_scatter | solution.py:51
  411.1 2.1 fusion.6
  413.6 129.4 %all_to_all.14 = bf16[8,192,1792]{2,1,0:T(8,128)(2,1)S(1)} all-to-all(bf16[8,192,1792]{2,1,0:T(8,128)(2,1)S(1)} %stack.2), channel_id=1, replica_groups=mesh['section'=4,'dp'=8,'tp'=8] {'dp'}, dimensions={0} | all-to-all | bytes 11010048 | tf_op jit(solution)/shard_map/all_to_all | solution.py:69
  543.0 4.7 fusion
  548.4 1.9 collective-permute-start
  551.0 2.9 collective-permute-done
  554.6 38.9 %reduce-scatter.5.cloned.1.call-done = f32[192,512]{1,0:T(8,128)} async-done(((f32[1536,512]{1,0:T(8,128)}), f32[192,512]{1,0:T(8,128)}) %reduce-scatter.5.cloned.1.call-update) | async-done | bytes 393232 | tf_op jit(solution)/shard_map/reduce_scatter | solution.py:74
  593.5 1.2 multiply_reduce_fusion
  594.7 14.2 %all-reduce.3 = (f32[192]{0:T(256)S(1)}, f32[192]{0:T(256)S(1)}) all-reduce(f32[192]{0:T(256)S(1)} %get-tuple-element.240, f32[192]{0:T(256)S(1)} %get-tuple-element.239), channel_id=1, replica_groups=mesh['section'=4,'dp'=8,'tp'=8] {'dp'}, use_global_device_ids=true, to_apply=%region_3.4 | all-reduce | flops 384 | bytes 3072 | tf_op jit(solution)/shard_map/psum | solution.py:79
  609.5 4.5 all-to-all-start.1
  615.0 1.3 bitcast_dynamic-update-slice_fusion
  616.3 2.9 all-to-all-done.1
  619.2 3.3 collective-permute-start.1
  622.6 2.1 collective-permute-done.1
  624.6 0.7 bitcast_subtract_fusion
  625.3 122.5 %while.31 = (s32[]{:T(128)}, f32[]{:T(128)}, f32[48]{0:T(128)S(1)}, f32[48]{0:T(128)S(1)}, f32[48]{0:T(128)S(1)}, /*index=5*/s32[]{:T(128)}, s32[]{:T(128)}) while((s32[]{:T(128)}, f32[]{:T(128)}, f32[48]{0:T(128)S(1)}, f32[48]{0:T(128)S(1)}, f32[48]{0:T(128)S(1)}, /*index=5*/s32[]{:T(128)}, s32[]{:T(128)}) %tuple.72), condition=%wide.region_7.8_spmd, body=%wide.region_6.7_spmd.sunk | while | flops 5 | bytes 157 | solution.py:104
  747.8 0.8 slice_dynamic-update-slice_fusion
  748.6 78.2 %all-reduce.2 = (f32[32]{0:T(128)S(1)}, f32[32]{0:T(128)S(1)}) all-reduce(f32[32]{0:T(128)S(1)} %slice_dynamic-update-slice_fusion, f32[32]{0:T(128)S(1)} %bitcast_dynamic-update-slice_fusion), channel_id=1, replica_groups=mesh['section'=4,'dp'=8,'tp'=8] {'section','tp'}, use_global_device_ids=true, to_apply=%add | all-reduce | flops 64 | bytes 512
  826.8 80.0 %while.32 = (s32[]{:T(128)}, f32[]{:T(128)}, s32[]{:T(128)}, f32[32]{0:T(128)S(1)}, f32[32]{0:T(128)S(1)}, /*index=5*/s32[]{:T(128)}, s32[]{:T(128)}, s32[]{:T(128)}, s32[]{:T(128)}) while((s32[]{:T(128)}, f32[]{:T(128)}, s32[]{:T(128)}, f32[32]{0:T(128)S(1)}, f32[32]{0:T(128)S(1)}, /*index=5*/s32[]{:T(128)}, s32[]{:T(128)}, s32[]{:T(128)}, ...), condition=%wide.region_10.11_spmd, body=%wide.region_9.10_spmd.sunk | while | flops 10 | bytes 217 | solution.py:33
  (248 shorter events, 106.2 us)
Async XLA Ops:
  7.2 161.6 %copy-start = (bf16[1,512,1792]{2,1,0:T(8,128)(2,1)S(1)}, bf16[1,512,1792]{2,1,0:T(8,128)(2,1)}, u32[]{:S(2)}) copy-start(bf16[1,512,1792]{2,1,0:T(8,128)(2,1)} %param.13) | copy-start | bytes 5505028
  7.2 160.1 %all-gather.3.cloned.1.call-start = ((), (), s32[]{:S(2)}) async-start(), calls=%async_computation.4 | async-start | bytes 1622016 | tf_op jit(solution)/shard_map/all_gather | solution.py:42
  7.9 403.2 %reduce-scatter.3.cloned.1.call-start = ((), (), s32[]{:S(2)}) async-start(), calls=%async_computation.5 | async-start | bytes 24772608 | tf_op jit(solution)/shard_map/reduce_scatter | solution.py:51
  168.8 3.0 copy-start.4
  182.9 410.6 %reduce-scatter.5.cloned.1.call-start = ((), (), s32[]{:S(2)}) async-start(), calls=%async_computation.6 | async-start | bytes 3538944 | tf_op jit(solution)/shard_map/reduce_scatter | solution.py:74
  413.6 129.4 %copy-start.5 = (bf16[1,1792,512]{2,1,0:T(8,128)(2,1)S(1)}, bf16[1,1792,512]{2,1,0:T(8,128)(2,1)}, u32[]{:S(2)}) copy-start(bf16[1,1792,512]{2,1,0:T(8,128)(2,1)} %param.14) | copy-start | bytes 5505028
  547.7 0.7 copy-start.3
  547.7 2.7 copy-start.2
  547.7 2.7 copy-start.6
  547.7 359.6 %copy-start.1 = (bf16[1,512,1792]{2,1,0:T(8,128)(2,1)S(1)}, bf16[1,512,1792]{2,1,0:T(8,128)(2,1)}, u32[]{:S(2)}) copy-start(bf16[1,512,1792]{2,1,0:T(8,128)(2,1)} %param.13) | copy-start | bytes 5505028
  548.4 5.5 collective-permute-start
  609.5 9.6 %all-to-all-start.1 = ((f32[4,1,48]{2,1,0:T(1,128)}), f32[4,1,48]{2,1,0:T(1,128)S(1)}, u32[]{:S(2)}, u32[]{:S(2)}) async-start(f32[4,1,48]{2,1,0:T(1,128)} %all_to_all.10), calls=%async_computation.3 | async-start | bytes 4096 | tf_op jit(solution)/shard_map/all_to_all | solution.py:83
  619.2 5.4 collective-permute-start.1
Sparse Core Ops, SparseCore 0:
  9.8 157.3 all-gather.2
  183.0 228.0 reduce-scatter.2
  547.9 45.5 reduce-scatter.4
